TPU v7x, 32 devices: a whole 2x2x4 slice. The times are simulated.
32 devices in a mesh: parts: 2 (over y), band: 4 (over z), win: 2 (over x), rep: 2 (over core).
Axes of the slice: x: 2, y: 2, z: 4, core: 2. Of those that a mesh axis runs over, the one named last changes fastest.
Arguments:
- records: bfloat16 [8, 15360, 512], P(('parts', 'win'), 'rep', 'band'), parts along dimension 0, may hold values from -30 to 30
- bin_first: int32 [1], replicated, may hold values from 56 to 66
- pair_blocks: int32 [4, 4, 2], P('band'), may hold values from 0 to 3, as said below
- pair_counts: int32 [4], P('band'), may hold values from 1 to 4
Outputs:
- cross: float32 [1088, 4, 128, 256], P(('parts', 'band'), 'rep', 'win'), parts along dimension 0
There are 2 independent parts, one for each index of `parts`. A program takes and returns all parts, laid end to end along the dimension named above; an argument that names none is the same for every part. Nothing has to cross between parts.
Inputs may be any that keep to these rules, and one draw needn't show every extreme that they name: `pair_blocks`: row s of band b names blocks i <= j of the 4 channel blocks with j - i <= 8.
All inputs are finite; a program needn't handle non-finite values.
Results may differ from a plain program's by a relative error of at most 0.015.
Values may be sent and summed in bfloat16 or wider, within the bound.
A program may use at most 128 MiB of HBM per device.

v0:
```python
import math

import jax
import jax.numpy as jnp
from jax import lax
from jax.sharding import PartitionSpec as P

SAMPLES = 15360
NBINS = 544
BLOCK = 128


water_level = 0.1


def dft_basis(start, rows, first, nbins, samples):
    times = start + lax.iota(jnp.int32, rows)
    freqs = first + lax.iota(jnp.int32, nbins)
    phase_index = times[:, None] * freqs[None, :] % samples
    phase = phase_index.astype(jnp.float32) * (2.0 * math.pi / samples)
    return jnp.concatenate([jnp.cos(phase), -jnp.sin(phase)], axis=1).astype(jnp.bfloat16)


def whiten(spectrum):
    count, doubled, width = spectrum.shape
    nbins = doubled // 2
    split = spectrum.reshape(count, 2, nbins, width)
    power = split[:, 0] * split[:, 0] + split[:, 1] * split[:, 1]
    level = jnp.sqrt(jnp.mean(power, axis=1) + 1e-06)
    denom = jnp.sqrt(power) + water_level * level[:, None, :]
    return split / denom[:, None]


def cross_terms(left, right, groups, total):
    count = left.shape[0]
    per_group = count // groups
    nbins = left.shape[2]
    rotated = jnp.stack(
        [
            jnp.concatenate([right[:, 0], -right[:, 1]], axis=-1),
            jnp.concatenate([right[:, 1], right[:, 0]], axis=-1),
        ],
        axis=1,
    )
    left_groups = left.reshape(groups, per_group, 2, nbins, left.shape[3])
    right_groups = rotated.reshape(groups, per_group, 2, nbins, rotated.shape[3])
    return (
        jnp.einsum(
            "gwpfr,gwpfc->gfrc", left_groups, right_groups, preferred_element_type=jnp.float32
        )
        / total
    )


def shards(records, bin_first, pair_blocks, pair_counts):
    win_local, half_rows, chan_local = records.shape
    rows = 1280
    row_base = lax.axis_index("rep") * half_rows
    first = bin_first[0]

    def step(carry, index):
        begin = index * rows
        basis = dft_basis(row_base + begin, rows, first, NBINS, SAMPLES)
        piece = lax.dynamic_slice_in_dim(records, begin, rows, 1)
        update = jnp.einsum("wtc,tk->wkc", piece, basis, preferred_element_type=jnp.float32)
        return (carry + update, None)

    start = jnp.zeros((win_local, 2 * NBINS, chan_local), jnp.float32)
    partial_value, _ = lax.scan(step, start, jnp.arange(half_rows // rows, dtype=jnp.int32))
    summed = lax.psum(partial_value.astype(jnp.bfloat16), "rep").astype(jnp.float32)
    white = whiten(summed).astype(jnp.bfloat16)
    moved = lax.all_to_all(white[:, :, :, None, :], "band", split_axis=2, concat_axis=3, tiled=True)
    band_bins = moved.shape[2]
    band_spec = moved.reshape(win_local, 2, band_bins, moved.shape[3] * moved.shape[4])
    slots = pair_blocks.shape[1] // lax.axis_size("rep")
    first_slot = lax.axis_index("rep") * slots
    mine = lax.dynamic_slice_in_dim(pair_blocks[0], first_slot, slots, 0)
    live_count = pair_counts[0]
    groups = lax.axis_size("win")
    total = win_local * groups
    everything = lax.all_gather(band_spec, "win", axis=0, tiled=True)
    share = BLOCK // groups
    offset = lax.axis_index("win") * share
    results = []
    for slot in range(slots):
        left = lax.dynamic_slice_in_dim(everything, mine[slot, 0] * BLOCK + offset, share, 3)
        right = lax.dynamic_slice_in_dim(everything, mine[slot, 1] * BLOCK, BLOCK, 3)
        term = cross_terms(left, right, groups, total)
        rounded = lax.optimization_barrier(term.astype(jnp.bfloat16))
        summed_groups = jnp.sum(rounded.astype(jnp.float32), axis=0)
        live = (first_slot + slot < live_count).astype(jnp.float32)
        results.append(summed_groups * live)
    return jnp.stack(results, axis=1)


def solution(mesh):
    return jax.shard_map(
        shards,
        mesh=mesh,
        in_specs=(P(("parts", "win"), "rep", "band"), P(), P("band", None, None), P("band")),
        out_specs=P(("parts", "band"), "rep", "win", None),
        check_vma=False,
    )
```

profile of v0, /device:TPU:0, one launch (start us, length us, event | category | flops | bytes accessed | tf_op | source)
XLA Modules:
  0.0 225.3 jit_solution(8368164281747097176)
XLA Ops:
  6.5 0.0 copy-start
  6.5 0.0 all-reduce.2.cloned.1.call-start
  6.5 97.0 %while.13 = (s32[]{:T(128)}, f32[2,1088,128]{2,1,0:T(8,128)S(1)}, s32[6]{0:T(128)S(1)}, s32[]{:T(128)}, s32[]{:T(128)}, /*index=5*/bf16[2,7680,128]{2,1,0:T(8,12...) while((s32[]{:T(128)}, f32[2,1088,128]{2,1,0:T(8,128)S(1)}, s32[6]{0:T(128)S(1)}, s32[]{:T(128)}, ...), condition=%wide.region_1.2_spmd.clone, body=%wide.region_0.1_spmd.clone.sunk | while | flops 727516992 | bytes 8468937 | solution.py:69
  6.5 0.7 dynamic_slice.46
  7.9 0.7 iota_add_fusion.4
  8.6 11.8 %cosine_convert_fusion.2 = (bf16[1280,544]{0,1:T(8,128)(2,1)S(1)}, bf16[1280,544]{0,1:T(8,128)(2,1)S(1)}) fusion(s32[544]{0:T(1024)S(1)} %iota_add_fusion.4, s32[1280]{0:T(1024)S(1)} %iota_add_fusion.5), kind=kLoop, calls=%fused_computation.8.clone.1 | loop fusion | flops 8355840 | bytes 2792576 | tf_op jit(solution)/shard_map/convert
  20.4 2.3 %fusion.41 = f32[2,1088,128]{2,1,0:T(8,128)S(1)} fusion(bf16[1280,544]{0,1:T(8,128)(2,1)S(1)} %get-tuple-element.174, bf16[1280,544]{0,1:T(8,128)(2,1)S(1)} %get-tuple-element.175, f32[2,1088,128]{2,1,0:T(8,128)S(1)} %get-tuple-element.187, bf16[2,7680,128]{2,1,0:T(8,128)(2,1)} %get-tuple-element.201, s32[]{:T(128)S(6)} %select_n.52, pred[]{:T(512)S(6)} %compare.3), kind=kOutput, calls=%fused_computation.14.clone.1 | convolution fusion | flops 719159296 | bytes 5668869 | tf_op jit(solution)/shard_map/while/body/eval_jaxpr/wtc,tk->wkc/dot_general | solution.py:65
  22.7 0.7 dynamic_slice.46
  24.1 0.7 iota_add_fusion.4
  24.8 11.8 %cosine_convert_fusion.2 = (bf16[1280,544]{0,1:T(8,128)(2,1)S(1)}, bf16[1280,544]{0,1:T(8,128)(2,1)S(1)}) fusion(s32[544]{0:T(1024)S(1)} %iota_add_fusion.4, s32[1280]{0:T(1024)S(1)} %iota_add_fusion.5), kind=kLoop, calls=%fused_computation.8.clone.1 | loop fusion | flops 8355840 | bytes 2792576 | tf_op jit(solution)/shard_map/convert
  36.6 2.3 %fusion.41 = f32[2,1088,128]{2,1,0:T(8,128)S(1)} fusion(bf16[1280,544]{0,1:T(8,128)(2,1)S(1)} %get-tuple-element.174, bf16[1280,544]{0,1:T(8,128)(2,1)S(1)} %get-tuple-element.175, f32[2,1088,128]{2,1,0:T(8,128)S(1)} %get-tuple-element.187, bf16[2,7680,128]{2,1,0:T(8,128)(2,1)} %get-tuple-element.201, s32[]{:T(128)S(6)} %select_n.52, pred[]{:T(512)S(6)} %compare.3), kind=kOutput, calls=%fused_computation.14.clone.1 | convolution fusion | flops 719159296 | bytes 5668869 | tf_op jit(solution)/shard_map/while/body/eval_jaxpr/wtc,tk->wkc/dot_general | solution.py:65
  38.9 0.7 dynamic_slice.46
  40.3 0.7 iota_add_fusion.4
  40.9 11.8 %cosine_convert_fusion.2 = (bf16[1280,544]{0,1:T(8,128)(2,1)S(1)}, bf16[1280,544]{0,1:T(8,128)(2,1)S(1)}) fusion(s32[544]{0:T(1024)S(1)} %iota_add_fusion.4, s32[1280]{0:T(1024)S(1)} %iota_add_fusion.5), kind=kLoop, calls=%fused_computation.8.clone.1 | loop fusion | flops 8355840 | bytes 2792576 | tf_op jit(solution)/shard_map/convert
  52.8 2.3 %fusion.41 = f32[2,1088,128]{2,1,0:T(8,128)S(1)} fusion(bf16[1280,544]{0,1:T(8,128)(2,1)S(1)} %get-tuple-element.174, bf16[1280,544]{0,1:T(8,128)(2,1)S(1)} %get-tuple-element.175, f32[2,1088,128]{2,1,0:T(8,128)S(1)} %get-tuple-element.187, bf16[2,7680,128]{2,1,0:T(8,128)(2,1)} %get-tuple-element.201, s32[]{:T(128)S(6)} %select_n.52, pred[]{:T(512)S(6)} %compare.3), kind=kOutput, calls=%fused_computation.14.clone.1 | convolution fusion | flops 719159296 | bytes 5668869 | tf_op jit(solution)/shard_map/while/body/eval_jaxpr/wtc,tk->wkc/dot_general | solution.py:65
  55.1 0.7 dynamic_slice.46
  56.4 0.7 iota_add_fusion.4
  57.1 11.8 %cosine_convert_fusion.2 = (bf16[1280,544]{0,1:T(8,128)(2,1)S(1)}, bf16[1280,544]{0,1:T(8,128)(2,1)S(1)}) fusion(s32[544]{0:T(1024)S(1)} %iota_add_fusion.4, s32[1280]{0:T(1024)S(1)} %iota_add_fusion.5), kind=kLoop, calls=%fused_computation.8.clone.1 | loop fusion | flops 8355840 | bytes 2792576 | tf_op jit(solution)/shard_map/convert
  68.9 2.3 %fusion.41 = f32[2,1088,128]{2,1,0:T(8,128)S(1)} fusion(bf16[1280,544]{0,1:T(8,128)(2,1)S(1)} %get-tuple-element.174, bf16[1280,544]{0,1:T(8,128)(2,1)S(1)} %get-tuple-element.175, f32[2,1088,128]{2,1,0:T(8,128)S(1)} %get-tuple-element.187, bf16[2,7680,128]{2,1,0:T(8,128)(2,1)} %get-tuple-element.201, s32[]{:T(128)S(6)} %select_n.52, pred[]{:T(512)S(6)} %compare.3), kind=kOutput, calls=%fused_computation.14.clone.1 | convolution fusion | flops 719159296 | bytes 5668869 | tf_op jit(solution)/shard_map/while/body/eval_jaxpr/wtc,tk->wkc/dot_general | solution.py:65
  71.2 0.7 dynamic_slice.46
  72.6 0.7 iota_add_fusion.4
  73.3 11.8 %cosine_convert_fusion.2 = (bf16[1280,544]{0,1:T(8,128)(2,1)S(1)}, bf16[1280,544]{0,1:T(8,128)(2,1)S(1)}) fusion(s32[544]{0:T(1024)S(1)} %iota_add_fusion.4, s32[1280]{0:T(1024)S(1)} %iota_add_fusion.5), kind=kLoop, calls=%fused_computation.8.clone.1 | loop fusion | flops 8355840 | bytes 2792576 | tf_op jit(solution)/shard_map/convert
  85.1 2.3 %fusion.41 = f32[2,1088,128]{2,1,0:T(8,128)S(1)} fusion(bf16[1280,544]{0,1:T(8,128)(2,1)S(1)} %get-tuple-element.174, bf16[1280,544]{0,1:T(8,128)(2,1)S(1)} %get-tuple-element.175, f32[2,1088,128]{2,1,0:T(8,128)S(1)} %get-tuple-element.187, bf16[2,7680,128]{2,1,0:T(8,128)(2,1)} %get-tuple-element.201, s32[]{:T(128)S(6)} %select_n.52, pred[]{:T(512)S(6)} %compare.3), kind=kOutput, calls=%fused_computation.14.clone.1 | convolution fusion | flops 719159296 | bytes 5668869 | tf_op jit(solution)/shard_map/while/body/eval_jaxpr/wtc,tk->wkc/dot_general | solution.py:65
  87.4 0.7 dynamic_slice.46
  88.8 0.7 iota_add_fusion.4
  89.5 11.8 %cosine_convert_fusion.2 = (bf16[1280,544]{0,1:T(8,128)(2,1)S(1)}, bf16[1280,544]{0,1:T(8,128)(2,1)S(1)}) fusion(s32[544]{0:T(1024)S(1)} %iota_add_fusion.4, s32[1280]{0:T(1024)S(1)} %iota_add_fusion.5), kind=kLoop, calls=%fused_computation.8.clone.1 | loop fusion | flops 8355840 | bytes 2792576 | tf_op jit(solution)/shard_map/convert
  101.3 2.3 %fusion.41 = f32[2,1088,128]{2,1,0:T(8,128)S(1)} fusion(bf16[1280,544]{0,1:T(8,128)(2,1)S(1)} %get-tuple-element.174, bf16[1280,544]{0,1:T(8,128)(2,1)S(1)} %get-tuple-element.175, f32[2,1088,128]{2,1,0:T(8,128)S(1)} %get-tuple-element.187, bf16[2,7680,128]{2,1,0:T(8,128)(2,1)} %get-tuple-element.201, s32[]{:T(128)S(6)} %select_n.52, pred[]{:T(512)S(6)} %compare.3), kind=kOutput, calls=%fused_computation.14.clone.1 | convolution fusion | flops 719159296 | bytes 5668869 | tf_op jit(solution)/shard_map/while/body/eval_jaxpr/wtc,tk->wkc/dot_general | solution.py:65
  103.6 0.9 convert_element_type.44
  104.5 0.0 all-reduce.2.cloned.1.call-update
  104.5 0.0 all-gather.2.cloned.1.call-start
  104.5 21.6 %all-reduce.2.cloned.1.call-done = bf16[2,1088,128]{2,1,0:T(8,128)(2,1)} async-done(((bf16[2,1088,128]{2,1,0:T(8,128)(2,1)}), bf16[2,1088,128]{2,1,0:T(8,128)(2,1)}) %all-reduce.2.cloned.1.call-update) | async-done | bytes 557072 | tf_op jit(solution)/shard_map/psum | solution.py:70
  126.1 1.1 convert_element_type.45
  127.3 0.1 fusion.34
  127.4 0.2 add_bitcast_fusion
  127.6 0.1 divide_convert_fusion
  127.7 0.4 copy.56
  128.1 20.3 %all_to_all.15 = bf16[2,2,544,1,128]{4,1,0,3,2:T(2,128)(2,1)S(1)} all-to-all(bf16[2,2,544,1,128]{4,1,0,3,2:T(2,128)(2,1)S(1)} %copy.56), channel_id=1, replica_groups=mesh['parts'=2,'band'=4,'win'=2,'rep'=2] {'band'}, dimensions={2} | all-to-all | bytes 1114112 | tf_op jit(solution)/shard_map/all_to_all | solution.py:72
  148.5 0.1 copy.57
  148.5 0.2 copy.58
  148.8 1.0 reshape.115
  149.8 0.0 all-gather.2.cloned.1.call-update
  149.8 0.0 copy-done
  149.8 0.1 constant_dynamic-slice_fusion.6
  149.9 0.1 copy.59
  150.0 0.7 fusion.37
  153.8 17.2 %all-gather.2.cloned.1.call-done = bf16[4,2,136,512]{3,2,1,0:T(8,128)(2,1)} async-done(((bf16[2,2,136,512]{3,2,1,0:T(8,128)(2,1)}), bf16[4,2,136,512]{3,2,1,0:T(8,128)(2,1)}) %all-gather.2.cloned.1.call-update) | async-done | bytes 1114128 | tf_op jit(solution)/shard_map/all_gather | solution.py:81
  171.0 0.0 copy-start.2
  171.0 1.3 constant_dynamic-slice_fusion.4
  172.3 0.1 copy.70
  172.4 0.1 copy.63
  172.5 0.2 copy_negate_fusion.1
  172.7 0.2 copy_negate_fusion
  172.9 0.0 copy-done.2
  172.9 0.2 constant_dynamic-slice_fusion.5
  173.2 5.3 %fusion.13 = bf16[2,136,64,256]{3,2,1,0:T(8,128)(2,1)} fusion(bf16[2,2,1,136,128]{4,1,2,3,0:T(2,128)(2,1)S(1)} %copy.70, bf16[2,2,1,136,128]{4,1,2,3,0:T(2,128)(2,1)S(1)} %get-tuple-element.128, bf16[2,2,1,136,128]{4,1,2,3,0:T(2,128)(2,1)S(1)} %get-tuple-element.127, bf16[2,2,2,136,64]{4,3,2,1,0:T(8,128)(2,1)S(1)} %bitcast.95), kind=kOutput, calls=%fused_computation.22 | convolution fusion | flops 46792704 | bytes 9469952 | tf_op jit(solution)/shard_map/gwpfr,gwpfc->gfrc/dot_general | solution.py:48
  178.5 10.2 %convert_reduce_fusion = f32[136,64,256]{2,1,0:T(8,128)} fusion(bf16[2,136,64,256]{3,2,1,0:T(8,128)(2,1)} %fusion.13), kind=kLoop, calls=%fused_computation.25 | loop fusion | flops 6684672 | bytes 17825792 | tf_op jit(solution)/shard_map/reduce_sum | solution.py:90
  188.7 5.3 %fusion.14 = bf16[2,136,64,256]{3,2,1,0:T(8,128)(2,1)} fusion(bf16[2,2,1,136,128]{4,1,2,3,0:T(2,128)(2,1)S(1)} %copy.63, bf16[2,2,1,136,128]{4,1,2,3,0:T(2,128)(2,1)S(1)} %get-tuple-element.126, bf16[2,2,1,136,128]{4,1,2,3,0:T(2,128)(2,1)S(1)} %get-tuple-element.125, bf16[2,2,2,136,64]{4,3,2,1,0:T(8,128)(2,1)S(1)} %bitcast.94), kind=kOutput, calls=%fused_computation.24 | convolution fusion | flops 46792704 | bytes 9469952 | tf_op jit(solution)/shard_map/gwpfr,gwpfc->gfrc/dot_general | solution.py:48
  194.0 10.2 %convert_reduce_fusion.1 = f32[136,64,256]{2,1,0:T(8,128)} fusion(bf16[2,136,64,256]{3,2,1,0:T(8,128)(2,1)} %fusion.14), kind=kLoop, calls=%fused_computation.26 | loop fusion | flops 6684672 | bytes 17825792 | tf_op jit(solution)/shard_map/reduce_sum | solution.py:90
  204.2 7.2 %multiply_bitcast_fusion = (f32[136,1,64,256]{3,2,1,0:T(8,128)S(1)}, f32[136,1,64,256]{3,2,1,0:T(8,128)S(1)}) fusion(f32[136,64,256]{2,1,0:T(8,128)} %convert_reduce_fusion, f32[]{:T(128)S(6)} %convert_element_type.52, f32[136,64,256]{2,1,0:T(8,128)} %convert_reduce_fusion.1, f32[]{:T(128)S(6)} %convert_element_type.49), kind=kLoop, calls=%fused_computation.27 | loop fusion | flops 4456448 | bytes 35651592 | tf_op jit(solution)/shard_map/mul | solution.py:92
  211.4 0.0 copy-start.1
  211.4 7.0 %pad_maximum_fusion = f32[136,2,64,256]{3,2,1,0:T(8,128)} fusion(f32[136,1,64,256]{3,2,1,0:T(8,128)S(1)} %get-tuple-element.133, f32[136,1,64,256]{3,2,1,0:T(8,128)S(1)} %get-tuple-element.134), kind=kLoop, calls=%fused_computation.20 | loop fusion | flops 4456448 | bytes 35651584 | tf_op jit(solution)/shard_map/stack | solution.py:93
  218.4 0.0 copy-done.1
  (9 shorter events, 0.1 us)
Async XLA Ops:
  6.5 143.3 %copy-start = (s32[1,4,2]{1,2,0:T(2,128)S(1)}, s32[1,4,2]{1,2,0:T(2,128)}, u32[]{:S(2)}) copy-start(s32[1,4,2]{1,2,0:T(2,128)} %param.8) | copy-start | bytes 100
  6.5 119.6 %all-reduce.2.cloned.1.call-start = ((), (), s32[]{:S(2)}) async-start(), calls=%async_computation.1 | async-start | bytes 1114112 | tf_op jit(solution)/shard_map/psum | solution.py:70
  104.5 66.5 %all-gather.2.cloned.1.call-start = ((), (), s32[]{:S(2)}) async-start(), calls=%async_computation.2 | async-start | bytes 1671168 | tf_op jit(solution)/shard_map/all_gather | solution.py:81
  171.0 1.9 copy-start.2
  211.4 7.0 %copy-start.1 = (s32[1,4,2]{1,2,0:T(2,128)S(1)}, s32[1,4,2]{1,2,0:T(2,128)}, u32[]{:S(2)}) copy-start(s32[1,4,2]{1,2,0:T(2,128)} %param.8) | copy-start | bytes 100
Sparse Core Ops, SparseCore 0:
  104.6 21.4 all-reduce.1
  149.9 21.0 all-gather.1
where the time goes:
time: 226 us; the launch traced here: 225 us
  other arithmetic  112 us (50%)
  waiting for transfers between devices  38.9 us (17%)
  matrix products  24.4 us (11%)
  blocking collectives  20.3 us (9%)
  between operations  16.7 us (7%)
  local copies, waits for them, and re-layouts  8.29 us (4%)
  loops' own time  4.47 us (2%)
    another operation x6, other arithmetic  70.9 us
    psum x1, waiting for transfers between devices, shards(): lax.psum(partial_value.astype(jnp.bfloat16), 'rep').astype(jnp.float32)  21.6 us
    reduce_sum x2, other arithmetic, shards(): summed_groups = jnp.sum(rounded.astype(jnp.float32), axis=0)  20.4 us
    all_to_all x1, blocking collectives, shards(): lax.all_to_all(white[:, :, :, None, :], 'band', split_axis=2, concat_axis...  20.3 us
    all_gather x1, waiting for transfers between devices, shards(): everything = lax.all_gather(band_spec, 'win', axis=0, tiled=True)  17.2 us
    dot_general x6, matrix products, step(): jnp.einsum('wtc,tk->wkc', piece, basis, preferred_element_type=jnp.float32)  13.8 us
    dot_general x2, matrix products, cross_terms(): jnp.einsum('gwpfr,gwpfc->gfrc', left_groups, right_groups, preferred_elem...  10.7 us
    mul x1, other arithmetic, shards(): results.append(summed_groups * live)  7.23 us
  transfers between devices with their start and end apart: 2, of which 2 were waited for; matrix products, arithmetic and copies ran while one was open for 0% of the time, Pallas kernels for 0%

commit v1 on v0

v1 whole, which is shorter than its diff:
```python
import functools
import math

import jax
import jax.numpy as jnp
from jax import lax
from jax.experimental import pallas as pl
from jax.experimental.pallas import tpu as pltpu
from jax.sharding import PartitionSpec as P

SAMPLES = 15360
NBINS = 544
BLOCK = 128
LANES = 128
SUB = 8
ROWS = 1280
MESH = pl.DeviceIdType.MESH

water_level = 0.1


def rotor(times, freqs):
    turns = times * freqs
    turns = turns - jnp.round(turns * (1.0 / SAMPLES)) * float(SAMPLES)
    half = turns * (math.pi / SAMPLES)
    square = half * half
    sine = jnp.full_like(half, -1.0 / math.factorial(11))
    for n in (9, 7, 5, 3, 1):
        sine = sine * square + (-1.0) ** (n // 2) / math.factorial(n)
    sine = sine * half
    cosine = jnp.full_like(half, 1.0 / math.factorial(12))
    for n in (10, 8, 6, 4, 2, 0):
        cosine = cosine * square + (-1.0) ** (n // 2) / math.factorial(n)
    return 1.0 - 2.0 * sine * sine, -2.0 * sine * cosine


def spectra_kernel(
    dims, first_ref, records_ref, out_ref, rec, basis, twiddle, acc, part_out, part_in, white,
    load_sem, rep_sems, z_send, z_recv, x_send, x_recv, own_send, own_recv, fwd_send, fwd_recv,
):
    bands, wins, band_bins, groups, blocks, chunks = dims
    total_groups = bands * groups
    band = lax.axis_index("band")
    win = lax.axis_index("win")
    rep = lax.axis_index("rep")
    other = 1 - rep

    def load(block):
        rows = pl.ds(pl.multiple_of(block * ROWS, ROWS), ROWS)
        return pltpu.make_async_copy(
            records_ref.at[:, rows, :], rec.at[:, rows, :], load_sem.at[block]
        )

    for block in reversed(range(blocks)):
        load(block).start()

    barrier = pltpu.get_barrier_semaphore()
    pl.semaphore_signal(barrier, inc=1, device_id={"rep": other}, device_id_type=MESH)
    for step in range(1, bands):
        pl.semaphore_signal(
            barrier, inc=1, device_id={"band": (band + step) % bands}, device_id_type=MESH
        )
    for step in range(1, wins):
        pl.semaphore_signal(
            barrier, inc=1, device_id={"win": (win + step) % wins}, device_id_type=MESH
        )

    base = (rep * (blocks * ROWS)).astype(jnp.float32)
    lane = lax.broadcasted_iota(jnp.int32, (SUB, LANES), 1).astype(jnp.float32)
    row = lax.broadcasted_iota(jnp.int32, (SUB, LANES), 0)
    first = first_ref[0]

    def build(group, _):
        local = (group % groups) * SUB + row
        freqs = (first + (group // groups) * band_bins + local).astype(jnp.float32)
        real, imag = rotor(base + lane, freqs)
        if band_bins % SUB:
            real = jnp.where(local < band_bins, real, 0.0)
            imag = jnp.where(local < band_bins, imag, 0.0)
        turn_real, turn_imag = rotor(float(LANES), freqs)
        block_real, block_imag = rotor(float(ROWS), freqs)
        twiddle[0, group] = block_real
        twiddle[1, group] = block_imag
        rows = pl.ds(pl.multiple_of(group * 2 * SUB, 2 * SUB), 2 * SUB)
        for part in range(ROWS // LANES):
            basis[rows, part * LANES : (part + 1) * LANES] = jnp.concatenate(
                [real, imag], axis=0
            ).astype(jnp.bfloat16)
            real, imag = (
                real * turn_real - imag * turn_imag,
                real * turn_imag + imag * turn_real,
            )
        return 0

    lax.fori_loop(0, total_groups, build, 0, unroll=2)
    acc[...] = jnp.zeros_like(acc)
    span = total_groups // chunks

    def transform(index, _):
        block = blocks - 1 - index
        load(block).wait()
        rows = pl.ds(pl.multiple_of(block * ROWS, ROWS), ROWS)
        both = jnp.concatenate([rec[0, rows, :], rec[1, rows, :]], axis=1)
        for chunk in range(chunks):
            product = jnp.dot(
                basis[chunk * span * 2 * SUB : (chunk + 1) * span * 2 * SUB, :],
                both,
                preferred_element_type=jnp.float32,
            ).reshape(span, 2, SUB, 2 * LANES)
            here = slice(chunk * span, (chunk + 1) * span)
            turn_real = twiddle[0, here]
            turn_imag = twiddle[1, here]
            for window in range(2):
                lanes = slice(window * LANES, (window + 1) * LANES)
                real = acc[window, here, 0]
                imag = acc[window, here, 1]
                acc[window, here, 0] = product[:, 0, :, lanes] + (
                    real * turn_real - imag * turn_imag
                )
                acc[window, here, 1] = product[:, 1, :, lanes] + (
                    real * turn_imag + imag * turn_real
                )
        return 0

    lax.fori_loop(0, blocks, transform, 0)
    part_out[...] = acc[other].reshape(part_out.shape).astype(jnp.bfloat16)
    pl.semaphore_wait(barrier, 1 + (bands - 1) + (wins - 1))
    exchange = pltpu.make_async_remote_copy(
        src_ref=part_out, dst_ref=part_in, send_sem=rep_sems.at[0], recv_sem=rep_sems.at[1],
        device_id={"rep": other}, device_id_type=MESH,
    )
    exchange.start()
    exchange.wait()

    spectrum = acc[rep] + part_in[...].astype(jnp.float32).reshape(total_groups, 2, SUB, LANES)
    acc[rep] = spectrum
    power = jnp.sum(jnp.sum(spectrum * spectrum, axis=1), axis=0)
    level = jnp.sqrt(jnp.sum(power, axis=0, keepdims=True) * (1.0 / NBINS) + 1e-06)
    floor = jnp.broadcast_to(water_level * level, (SUB, LANES))

    def whiten(group, _):
        pair = acc[rep, group]
        real, imag = pair[0], pair[1]
        scale = 1.0 / (jnp.sqrt(real * real + imag * imag) + floor)
        rows = pl.ds(pl.multiple_of((group % groups) * 2 * SUB, 2 * SUB), 2 * SUB)
        white[group // groups, rows, :] = jnp.concatenate(
            [real * scale, imag * scale], axis=0
        ).astype(jnp.bfloat16)
        return 0

    lax.fori_loop(0, total_groups, whiten, 0, unroll=4)

    mine = win * 2 + rep

    def to_band(step):
        target = (band + step) % bands
        return pltpu.make_async_remote_copy(
            src_ref=white.at[target], dst_ref=out_ref.at[mine, band],
            send_sem=z_send.at[step], recv_sem=z_recv.at[step],
            device_id={"band": target}, device_id_type=MESH,
        )

    def to_win(step, hop, source):
        return pltpu.make_async_remote_copy(
            src_ref=out_ref.at[mine, source], dst_ref=out_ref.at[mine, source],
            send_sem=x_send.at[hop, step], recv_sem=x_recv.at[hop, step],
            device_id={"win": (win + hop) % wins}, device_id_type=MESH,
        )

    def to_rep(step, source):
        return pltpu.make_async_remote_copy(
            src_ref=out_ref.at[mine, source], dst_ref=out_ref.at[mine, source],
            send_sem=own_send.at[step], recv_sem=own_recv.at[step],
            device_id={"rep": other}, device_id_type=MESH,
        )

    def forward(step, hop, source):
        window = ((win - hop + wins) % wins) * 2 + rep
        return pltpu.make_async_remote_copy(
            src_ref=out_ref.at[window, source], dst_ref=out_ref.at[window, source],
            send_sem=fwd_send.at[hop, step], recv_sem=fwd_recv.at[hop, step],
            device_id={"rep": other}, device_id_type=MESH,
        )

    for step in range(1, bands):
        to_band(step).start()
    out_ref[mine, band] = white[band]
    for step in range(bands):
        source = (band - step + bands) % bands
        if step:
            to_band(step).wait_recv()
        for hop in range(1, wins):
            to_win(step, hop, source).start()
        to_rep(step, source).start()
        if step:
            last = (band - step + 1 + bands) % bands
            for hop in range(1, wins):
                to_win(step - 1, hop, last).wait_recv()
                forward(step - 1, hop, last).start()
    last = (band + 1) % bands
    for hop in range(1, wins):
        to_win(bands - 1, hop, last).wait_recv()
        forward(bands - 1, hop, last).start()
    for step in range(bands):
        source = (band - step + bands) % bands
        if step:
            to_band(step).wait_send()
        to_rep(step, source).wait()
        for hop in range(1, wins):
            to_win(step, hop, source).wait_send()
            forward(step, hop, source).wait()


def cross_kernel(windows, share, slots, pairs_ref, counts_ref, white_ref, out_ref):
    rep = lax.axis_index("rep")
    shift = lax.axis_index("win") * share
    group = pl.program_id(0)
    rows = pl.ds(pl.multiple_of(group * 2 * SUB, 2 * SUB), 2 * SUB)
    depth = windows * 2 * SUB
    bins = lax.broadcasted_iota(jnp.int32, (share, depth), 1) % SUB
    for slot in range(slots):
        place = rep * slots + slot
        scale = jnp.where(place < counts_ref[0], 1.0 / windows, 0.0).astype(jnp.float32)
        left = white_ref[:, pairs_ref[0, place, 0], rows, :].reshape(depth, BLOCK)
        left = left.astype(jnp.float32) * scale
        left = pltpu.roll(left, (BLOCK - shift) % BLOCK, 1)
        left = left.T[:share, :]
        spread = jnp.concatenate(
            [jnp.where(bins == index, left, 0.0) for index in range(SUB)], axis=0
        ).astype(jnp.bfloat16)
        right = white_ref[:, pairs_ref[0, place, 1], rows, :].astype(jnp.float32)
        turned = jnp.concatenate([-right[:, SUB:], right[:, :SUB]], axis=1)
        both = jnp.concatenate(
            [right.reshape(depth, BLOCK), turned.reshape(depth, BLOCK)], axis=1
        ).astype(jnp.bfloat16)
        out_ref[:, slot] = jnp.dot(spread, both, preferred_element_type=jnp.float32).reshape(
            SUB, share, 2 * BLOCK
        )


def shards(bands, wins, records, bin_first, pair_blocks, pair_counts):
    _, half_rows, _ = records.shape
    band_bins = NBINS // bands
    groups = -(-band_bins // SUB)
    blocks = half_rows // ROWS
    total_groups = bands * groups
    chunks = 2
    windows = wins * 2
    doubled = groups * 2 * SUB
    slots = pair_blocks.shape[1] // 2
    share = BLOCK // wins
    dma = pltpu.SemaphoreType.DMA
    everything = pl.pallas_call(
        functools.partial(spectra_kernel, (bands, wins, band_bins, groups, blocks, chunks)),
        out_shape=jax.ShapeDtypeStruct((windows, bands, doubled, LANES), jnp.bfloat16),
        in_specs=[pl.BlockSpec(memory_space=pltpu.SMEM), pl.BlockSpec(memory_space=pl.ANY)],
        out_specs=pl.BlockSpec(memory_space=pltpu.VMEM),
        scratch_shapes=[
            pltpu.VMEM((2, half_rows, LANES), jnp.bfloat16),
            pltpu.VMEM((total_groups * 2 * SUB, ROWS), jnp.bfloat16),
            pltpu.VMEM((2, total_groups, SUB, LANES), jnp.float32),
            pltpu.VMEM((2, total_groups, 2, SUB, LANES), jnp.float32),
            pltpu.VMEM((total_groups * 2 * SUB, LANES), jnp.bfloat16),
            pltpu.VMEM((total_groups * 2 * SUB, LANES), jnp.bfloat16),
            pltpu.VMEM((bands, doubled, LANES), jnp.bfloat16),
            dma((blocks,)),
            dma((2,)),
            dma((bands,)),
            dma((bands,)),
            dma((wins, bands)),
            dma((wins, bands)),
            dma((bands,)),
            dma((bands,)),
            dma((wins, bands)),
            dma((wins, bands)),
        ],
        compiler_params=pltpu.CompilerParams(
            collective_id=0, has_side_effects=True, vmem_limit_bytes=40 * 2**20
        ),
        name="spectra",
    )(bin_first, records)
    return pl.pallas_call(
        functools.partial(cross_kernel, windows, share, slots),
        out_shape=jax.ShapeDtypeStruct((band_bins, slots, share, 2 * BLOCK), jnp.float32),
        grid_spec=pltpu.PrefetchScalarGridSpec(
            num_scalar_prefetch=2,
            grid=(groups,),
            in_specs=[pl.BlockSpec(memory_space=pltpu.VMEM)],
            out_specs=pl.BlockSpec((SUB, slots, share, 2 * BLOCK), lambda g, *_: (g, 0, 0, 0)),
        ),
        compiler_params=pltpu.CompilerParams(vmem_limit_bytes=40 * 2**20),
        name="cross",
    )(pair_blocks, pair_counts, everything)


def solution(mesh):
    return jax.shard_map(
        functools.partial(shards, mesh.shape["band"], mesh.shape["win"]),
        mesh=mesh,
        in_specs=(P(("parts", "win"), "rep", "band"), P(), P("band", None, None), P("band")),
        out_specs=P(("parts", "band"), "rep", "win", None),
        check_vma=False,
    )
```

time: 226 us -> 44.6 us (0.20)
  other arithmetic: 112 us -> 0 us
  Pallas kernels: 0 us -> 40.3 us
  waiting for transfers between devices: 38.9 us -> 0 us
  matrix products: 24.4 us -> 0 us
  blocking collectives: 20.3 us -> 0 us
  between operations: 16.7 us -> 1.31 us
  local copies, waits for them, and re-layouts: 8.29 us -> 2.88 us
  loops' own time: 4.47 us -> 0 us
    another operation x7 -> x0, other arithmetic: 77.9 us -> none
    pallas_call x0 -> x2, Pallas kernels: none -> 40.3 us  [the longest x1 27.3 us: shards(): pl.pallas_call(functools.partial(spectra_kernel, (bands, wins, band_bins,...]
    dot_general x8 -> x0, matrix products: 24.4 us -> none  [the longest x6 13.8 us: step(): jnp.einsum('wtc,tk->wkc', piece, basis, preferred_element_type=jnp.float32)]
    psum x1 -> x0, waiting for transfers between devices: 21.6 us -> none  [shards(): lax.psum(partial_value.astype(jnp.bfloat16), 'rep').astype(jnp.float32)]
    reduce_sum x3 -> x0, other arithmetic: 20.5 us -> none  [the longest x2 20.4 us: shards(): summed_groups = jnp.sum(rounded.astype(jnp.float32), axis=0)]
    all_to_all x1 -> x0, blocking collectives: 20.3 us -> none  [shards(): lax.all_to_all(white[:, :, :, None, :], 'band', split_axis=2, concat_axis...]
    all_gather x1 -> x0, waiting for transfers between devices: 17.2 us -> none  [shards(): everything = lax.all_gather(band_spec, 'win', axis=0, tiled=True)]
    mul x2 -> x0, other arithmetic: 7.24 us -> none  [the longest x1 7.23 us: shards(): results.append(summed_groups * live)]
  transfers between devices with their start and end apart: 2 -> 0, of which waited for: 2 -> 0; matrix products, arithmetic and copies ran while one was open for 0% -> 0% of each run, Pallas kernels for 0% -> 0%
where the time goes in v1:
time: 44.6 us; the launch traced here: 44.5 us
  Pallas kernels  40.3 us (90%)
  local copies, waits for them, and re-layouts  2.88 us (6%)
  between operations  1.31 us (3%)
    pallas_call x1, Pallas kernels, shards(): pl.pallas_call(functools.partial(spectra_kernel, (bands, wins, band_bins,...  27.3 us
    pallas_call x1, Pallas kernels, shards(): pl.pallas_call(functools.partial(cross_kernel, windows, share, slots), ou...  13 us
    unnamed x3, local copies, waits for them, and re-layouts  2.88 us

profile of v1, /device:TPU:0, one launch (start us, length us, event | category | flops | bytes accessed | tf_op | source)
XLA Modules:
  0.0 44.5 jit_solution(8402204850071660518)
XLA Ops:
  1.3 0.8 %copy.5.pairs_ref = s32[1,4,2]{2,1,0:T(4,128)S(1)} copy(s32[1,4,2]{1,2,0:T(2,128)} %param.6) | data formatting | bytes 64 | tf_op args[2]
  2.1 0.0 copy-start
  2.1 2.1 %copy-done = bf16[2,7680,128]{2,1,0:T(8,128)(2,1)S(1)} copy-done((bf16[2,7680,128]{2,1,0:T(8,128)(2,1)S(1)}, bf16[2,7680,128]{2,1,0:T(8,128)(2,1)}, u32[]{:S(2)}) %copy-start) | copy-done | bytes 3932184
  4.2 27.3 %spectra.1.white_ref = bf16[4,4,272,128]{3,2,1,0:T(8,128)(2,1)S(1)} custom-call(s32[1]{0:T(128)S(6)} %copy.6.first_ref, bf16[2,7680,128]{2,1,0:T(8,128)(2,1)S(1)} %copy-done), custom_call_target="tpu_custom_call" | custom-call | tf_op jit(solution)/shard_map/spectra/pallas_call | solution.py:253
  31.4 13.0 %cross.1 = f32[136,2,64,256]{3,2,1,0:T(8,128)} custom-call(s32[1,4,2]{2,1,0:T(4,128)S(1)} %copy.5.pairs_ref, s32[1]{0:T(128)S(6)} %copy.7.counts_ref, bf16[4,4,272,128]{3,2,1,0:T(8,128)(2,1)S(1)} %spectra.1.white_ref), custom_call_target="tpu_custom_call" | custom-call | tf_op jit(solution)/shard_map/cross/pallas_call | solution.py:282
Async XLA Ops:
  2.1 2.1 %copy-start = (bf16[2,7680,128]{2,1,0:T(8,128)(2,1)S(1)}, bf16[2,7680,128]{2,1,0:T(8,128)(2,1)}, u32[]{:S(2)}) copy-start(bf16[2,7680,128]{2,1,0:T(8,128)(2,1)} %records_ref.1) | copy-start | bytes 11796484

commit v2 on v1

--- a/solution.py
+++ b/solution.py
@@ -14,6 +14,9 @@
 LANES = 128
 SUB = 8
 ROWS = 1280
+WIDE = 4
+PIECES = 3
+PER = 3
 MESH = pl.DeviceIdType.MESH
 
 water_level = 0.1
@@ -66,33 +69,37 @@
         )
 
     base = (rep * (blocks * ROWS)).astype(jnp.float32)
-    lane = lax.broadcasted_iota(jnp.int32, (SUB, LANES), 1).astype(jnp.float32)
-    row = lax.broadcasted_iota(jnp.int32, (SUB, LANES), 0)
+    lane = lax.broadcasted_iota(jnp.int32, (WIDE, SUB, LANES), 2).astype(jnp.float32)
+    row = lax.broadcasted_iota(jnp.int32, (WIDE, SUB, LANES), 1)
     first = first_ref[0]
 
-    def build(group, _):
-        local = (group % groups) * SUB + row
-        freqs = (first + (group // groups) * band_bins + local).astype(jnp.float32)
+    def build(index, _):
+        ids = index * WIDE + lax.broadcasted_iota(jnp.int32, (WIDE, SUB, LANES), 0)
+        local = (ids % groups) * SUB + row
+        freqs = (first + (ids // groups) * band_bins + local).astype(jnp.float32)
         real, imag = rotor(base + lane, freqs)
         if band_bins % SUB:
             real = jnp.where(local < band_bins, real, 0.0)
             imag = jnp.where(local < band_bins, imag, 0.0)
         turn_real, turn_imag = rotor(float(LANES), freqs)
         block_real, block_imag = rotor(float(ROWS), freqs)
-        twiddle[0, group] = block_real
-        twiddle[1, group] = block_imag
-        rows = pl.ds(pl.multiple_of(group * 2 * SUB, 2 * SUB), 2 * SUB)
+        here = pl.ds(index * WIDE, WIDE)
+        twiddle[0, here] = block_real
+        twiddle[1, here] = block_imag
+        rows = pl.ds(pl.multiple_of(index * (WIDE * 2 * SUB), WIDE * 2 * SUB), WIDE * 2 * SUB)
         for part in range(ROWS // LANES):
-            basis[rows, part * LANES : (part + 1) * LANES] = jnp.concatenate(
-                [real, imag], axis=0
-            ).astype(jnp.bfloat16)
+            basis[rows, part * LANES : (part + 1) * LANES] = (
+                jnp.concatenate([real, imag], axis=1)
+                .reshape(WIDE * 2 * SUB, LANES)
+                .astype(jnp.bfloat16)
+            )
             real, imag = (
                 real * turn_real - imag * turn_imag,
                 real * turn_imag + imag * turn_real,
             )
         return 0
 
-    lax.fori_loop(0, total_groups, build, 0, unroll=2)
+    lax.fori_loop(0, total_groups // WIDE, build, 0)
     acc[...] = jnp.zeros_like(acc)
     span = total_groups // chunks
 
@@ -152,90 +159,104 @@
 
     mine = win * 2 + rep
 
-    def to_band(step):
+    cuts = [2 * SUB * (groups * piece // PIECES) for piece in range(PIECES + 1)]
+
+    def span_of(piece):
+        return pl.ds(cuts[piece], cuts[piece + 1] - cuts[piece])
+
+    def source(step):
+        return (band - step + bands) % bands
+
+    def to_band(step, piece):
         target = (band + step) % bands
         return pltpu.make_async_remote_copy(
-            src_ref=white.at[target], dst_ref=out_ref.at[mine, band],
-            send_sem=z_send.at[step], recv_sem=z_recv.at[step],
+            src_ref=white.at[target, span_of(piece)],
+            dst_ref=out_ref.at[mine, band, span_of(piece)],
+            send_sem=z_send.at[step, piece], recv_sem=z_recv.at[step, piece],
             device_id={"band": target}, device_id_type=MESH,
         )
 
-    def to_win(step, hop, source):
+    def to_win(step, piece, hop):
+        block = out_ref.at[mine, source(step), span_of(piece)]
         return pltpu.make_async_remote_copy(
-            src_ref=out_ref.at[mine, source], dst_ref=out_ref.at[mine, source],
-            send_sem=x_send.at[hop, step], recv_sem=x_recv.at[hop, step],
+            src_ref=block, dst_ref=block,
+            send_sem=x_send.at[hop, step, piece], recv_sem=x_recv.at[hop, step, piece],
             device_id={"win": (win + hop) % wins}, device_id_type=MESH,
         )
 
-    def to_rep(step, source):
+    def to_rep(step, piece):
+        block = out_ref.at[mine, source(step), span_of(piece)]
         return pltpu.make_async_remote_copy(
-            src_ref=out_ref.at[mine, source], dst_ref=out_ref.at[mine, source],
-            send_sem=own_send.at[step], recv_sem=own_recv.at[step],
+            src_ref=block, dst_ref=block,
+            send_sem=own_send.at[step, piece], recv_sem=own_recv.at[step, piece],
             device_id={"rep": other}, device_id_type=MESH,
         )
 
-    def forward(step, hop, source):
+    def forward(step, piece, hop):
         window = ((win - hop + wins) % wins) * 2 + rep
+        block = out_ref.at[window, source(step), span_of(piece)]
         return pltpu.make_async_remote_copy(
-            src_ref=out_ref.at[window, source], dst_ref=out_ref.at[window, source],
-            send_sem=fwd_send.at[hop, step], recv_sem=fwd_recv.at[hop, step],
+            src_ref=block, dst_ref=block,
+            send_sem=fwd_send.at[hop, step, piece], recv_sem=fwd_recv.at[hop, step, piece],
             device_id={"rep": other}, device_id_type=MESH,
         )
 
-    for step in range(1, bands):
-        to_band(step).start()
-    out_ref[mine, band] = white[band]
-    for step in range(bands):
-        source = (band - step + bands) % bands
+    def relay(item):
+        step, piece = item
+        for hop in range(1, wins):
+            to_win(step, piece, hop).wait_recv()
+            forward(step, piece, hop).start()
+
+    for piece in range(PIECES):
+        for step in range(1, bands):
+            to_band(step, piece).start()
+    out_ref[mine, band, : cuts[-1]] = white[band]
+    items = [(0, piece) for piece in range(PIECES)]
+    items += [(step, piece) for piece in range(PIECES) for step in range(1, bands)]
+    for place, (step, piece) in enumerate(items):
         if step:
-            to_band(step).wait_recv()
+            to_band(step, piece).wait_recv()
         for hop in range(1, wins):
-            to_win(step, hop, source).start()
-        to_rep(step, source).start()
+            to_win(step, piece, hop).start()
+        to_rep(step, piece).start()
+        if place >= PIECES:
+            relay(items[place - PIECES])
+    for item in items[-PIECES:]:
+        relay(item)
+    for step, piece in items:
         if step:
-            last = (band - step + 1 + bands) % bands
-            for hop in range(1, wins):
-                to_win(step - 1, hop, last).wait_recv()
-                forward(step - 1, hop, last).start()
-    last = (band + 1) % bands
-    for hop in range(1, wins):
-        to_win(bands - 1, hop, last).wait_recv()
-        forward(bands - 1, hop, last).start()
-    for step in range(bands):
-        source = (band - step + bands) % bands
-        if step:
-            to_band(step).wait_send()
-        to_rep(step, source).wait()
+            to_band(step, piece).wait_send()
+        to_rep(step, piece).wait()
         for hop in range(1, wins):
-            to_win(step, hop, source).wait_send()
-            forward(step, hop, source).wait()
-
-
-def cross_kernel(windows, share, slots, pairs_ref, counts_ref, white_ref, out_ref):
+            to_win(step, piece, hop).wait_send()
+            forward(step, piece, hop).wait()
+
+
+def cross_kernel(windows, share, slots, per, pairs_ref, counts_ref, white_ref, out_ref):
     rep = lax.axis_index("rep")
     shift = lax.axis_index("win") * share
-    group = pl.program_id(0)
-    rows = pl.ds(pl.multiple_of(group * 2 * SUB, 2 * SUB), 2 * SUB)
     depth = windows * 2 * SUB
     bins = lax.broadcasted_iota(jnp.int32, (share, depth), 1) % SUB
-    for slot in range(slots):
-        place = rep * slots + slot
-        scale = jnp.where(place < counts_ref[0], 1.0 / windows, 0.0).astype(jnp.float32)
-        left = white_ref[:, pairs_ref[0, place, 0], rows, :].reshape(depth, BLOCK)
-        left = left.astype(jnp.float32) * scale
-        left = pltpu.roll(left, (BLOCK - shift) % BLOCK, 1)
-        left = left.T[:share, :]
-        spread = jnp.concatenate(
-            [jnp.where(bins == index, left, 0.0) for index in range(SUB)], axis=0
-        ).astype(jnp.bfloat16)
-        right = white_ref[:, pairs_ref[0, place, 1], rows, :].astype(jnp.float32)
-        turned = jnp.concatenate([-right[:, SUB:], right[:, :SUB]], axis=1)
-        both = jnp.concatenate(
-            [right.reshape(depth, BLOCK), turned.reshape(depth, BLOCK)], axis=1
-        ).astype(jnp.bfloat16)
-        out_ref[:, slot] = jnp.dot(spread, both, preferred_element_type=jnp.float32).reshape(
-            SUB, share, 2 * BLOCK
-        )
+    masks = [jnp.where(bins == index, 1.0, 0.0).astype(jnp.bfloat16) for index in range(SUB)]
+    for part in range(per):
+        start = (pl.program_id(0) * per + part) * 2 * SUB
+        rows = pl.ds(pl.multiple_of(start, 2 * SUB), 2 * SUB)
+        for slot in range(slots):
+            place = rep * slots + slot
+            scale = jnp.where(place < counts_ref[0], 1.0 / windows, 0.0).astype(jnp.float32)
+            left = white_ref[:, pairs_ref[0, 0, place], rows, :].reshape(depth, BLOCK)
+            left = left.astype(jnp.float32) * scale
+            left = pltpu.roll(left, (BLOCK - shift) % BLOCK, 1)
+            left = left.T[:share, :].astype(jnp.bfloat16)
+            spread = jnp.concatenate([left * mask for mask in masks], axis=0)
+            right = white_ref[:, pairs_ref[0, 1, place], rows, :].astype(jnp.float32)
+            turned = jnp.concatenate([-right[:, SUB:], right[:, :SUB]], axis=1)
+            both = jnp.concatenate(
+                [right.reshape(depth, BLOCK), turned.reshape(depth, BLOCK)], axis=1
+            ).astype(jnp.bfloat16)
+            out_ref[part * SUB : (part + 1) * SUB, slot] = jnp.dot(
+                spread, both, preferred_element_type=jnp.float32
+            ).reshape(SUB, share, 2 * BLOCK)
 
 
 def shards(bands, wins, records, bin_first, pair_blocks, pair_counts):
@@ -252,7 +273,7 @@
     dma = pltpu.SemaphoreType.DMA
     everything = pl.pallas_call(
         functools.partial(spectra_kernel, (bands, wins, band_bins, groups, blocks, chunks)),
-        out_shape=jax.ShapeDtypeStruct((windows, bands, doubled, LANES), jnp.bfloat16),
+        out_shape=jax.ShapeDtypeStruct((windows, bands, -(-groups // PER) * PER * 2 * SUB, LANES), jnp.bfloat16),
         in_specs=[pl.BlockSpec(memory_space=pltpu.SMEM), pl.BlockSpec(memory_space=pl.ANY)],
         out_specs=pl.BlockSpec(memory_space=pltpu.VMEM),
         scratch_shapes=[
@@ -265,32 +286,32 @@
             pltpu.VMEM((bands, doubled, LANES), jnp.bfloat16),
             dma((blocks,)),
             dma((2,)),
-            dma((bands,)),
-            dma((bands,)),
-            dma((wins, bands)),
-            dma((wins, bands)),
-            dma((bands,)),
-            dma((bands,)),
-            dma((wins, bands)),
-            dma((wins, bands)),
+            dma((bands, PIECES)),
+            dma((bands, PIECES)),
+            dma((wins, bands, PIECES)),
+            dma((wins, bands, PIECES)),
+            dma((bands, PIECES)),
+            dma((bands, PIECES)),
+            dma((wins, bands, PIECES)),
+            dma((wins, bands, PIECES)),
         ],
         compiler_params=pltpu.CompilerParams(
-            collective_id=0, has_side_effects=True, vmem_limit_bytes=40 * 2**20
+            collective_id=0, has_side_effects=True, vmem_limit_bytes=605 * 2**20 // 10
         ),
         name="spectra",
     )(bin_first, records)
     return pl.pallas_call(
-        functools.partial(cross_kernel, windows, share, slots),
+        functools.partial(cross_kernel, windows, share, slots, PER),
         out_shape=jax.ShapeDtypeStruct((band_bins, slots, share, 2 * BLOCK), jnp.float32),
         grid_spec=pltpu.PrefetchScalarGridSpec(
             num_scalar_prefetch=2,
-            grid=(groups,),
+            grid=(-(-groups // PER),),
             in_specs=[pl.BlockSpec(memory_space=pltpu.VMEM)],
-            out_specs=pl.BlockSpec((SUB, slots, share, 2 * BLOCK), lambda g, *_: (g, 0, 0, 0)),
+            out_specs=pl.BlockSpec((PER * SUB, slots, share, 2 * BLOCK), lambda g, *_: (g, 0, 0, 0)),
         ),
         compiler_params=pltpu.CompilerParams(vmem_limit_bytes=40 * 2**20),
         name="cross",
-    )(pair_blocks, pair_counts, everything)
+    )(jnp.swapaxes(pair_blocks, 1, 2), pair_counts, everything)
 
 
 def solution(mesh):

time: 44.6 us -> 40.1 us (0.90)
  Pallas kernels: 40.3 us -> 37.3 us
  local copies, waits for them, and re-layouts: 2.88 us -> 1.27 us
    pallas_call x1, Pallas kernels: 13 us -> 8.32 us  [shards(): pl.pallas_call(functools.partial(cross_kernel, windows, share, slots, PER...]
    pallas_call x1, Pallas kernels: 27.3 us -> 29 us  [shards(): pl.pallas_call(functools.partial(spectra_kernel, (bands, wins, band_bins,...]
    unnamed x3 -> x4, local copies, waits for them, and re-layouts: 2.88 us -> 1.27 us
where the time goes in v2:
time: 40.1 us; the launch traced here: 39.9 us
  Pallas kernels  37.3 us (93%)
  between operations  1.34 us (3%)
  local copies, waits for them, and re-layouts  1.27 us (3%)
    pallas_call x1, Pallas kernels, shards(): pl.pallas_call(functools.partial(spectra_kernel, (bands, wins, band_bins,...  29 us
    pallas_call x1, Pallas kernels, shards(): pl.pallas_call(functools.partial(cross_kernel, windows, share, slots, PER...  8.32 us
    unnamed x4, local copies, waits for them, and re-layouts  1.27 us

profile of v2, /device:TPU:0, one launch (start us, length us, event | category | flops | bytes accessed | tf_op | source)
XLA Modules:
  0.0 39.9 jit_solution(3736312818425464639)
XLA Ops:
  0.0 0.0 copy-start.1
  1.3 29.0 %spectra.1.white_ref = bf16[4,4,288,128]{3,2,1,0:T(8,128)(2,1)} custom-call(s32[1]{0:T(128)S(6)} %copy.5.first_ref, bf16[2,7680,128]{2,1,0:T(8,128)(2,1)} %records_ref.1), custom_call_target="tpu_custom_call" | custom-call | tf_op jit(solution)/shard_map/spectra/pallas_call | solution.py:274
  30.3 0.0 copy-done.1
  30.3 0.0 copy-start
  30.3 1.3 %copy-done = bf16[4,4,288,128]{3,2,1,0:T(8,128)(2,1)S(1)} copy-done((bf16[4,4,288,128]{3,2,1,0:T(8,128)(2,1)S(1)}, bf16[4,4,288,128]{3,2,1,0:T(8,128)(2,1)}, u32[]{:S(2)}) %copy-start) | copy-done | bytes 1179672
  31.6 8.3 %cross.1 = f32[136,2,64,256]{3,2,1,0:T(8,128)} custom-call(s32[1,2,4]{2,1,0:T(2,128)S(1)} %bitcast.1, s32[1]{0:T(128)S(6)} %copy.6.counts_ref, bf16[4,4,288,128]{3,2,1,0:T(8,128)(2,1)S(1)} %copy-done), custom_call_target="tpu_custom_call" | custom-call | tf_op jit(solution)/shard_map/cross/pallas_call | solution.py:303
Async XLA Ops:
  0.0 30.3 %copy-start.1 = (s32[1,4,2]{1,2,0:T(2,128)S(1)}, s32[1,4,2]{1,2,0:T(2,128)}, u32[]{:S(2)}) copy-start(s32[1,4,2]{1,2,0:T(2,128)} %param.6) | copy-start | bytes 100
  30.3 1.3 %copy-start = (bf16[4,4,288,128]{3,2,1,0:T(8,128)(2,1)S(1)}, bf16[4,4,288,128]{3,2,1,0:T(8,128)(2,1)}, u32[]{:S(2)}) copy-start(bf16[4,4,288,128]{3,2,1,0:T(8,128)(2,1)} %spectra.1.white_ref) | copy-start | bytes 3538948

commit v3 on v2

--- a/solution.py
+++ b/solution.py
@@ -15,7 +15,9 @@
 SUB = 8
 ROWS = 1280
 WIDE = 4
-PIECES = 3
+PIECES = 1
+AHEAD = 1
+LAG = 3
 PER = 3
 MESH = pl.DeviceIdType.MESH
 
@@ -207,7 +209,7 @@
             to_win(step, piece, hop).wait_recv()
             forward(step, piece, hop).start()
 
-    for piece in range(PIECES):
+    for piece in range(min(AHEAD, PIECES)):
         for step in range(1, bands):
             to_band(step, piece).start()
     out_ref[mine, band, : cuts[-1]] = white[band]
@@ -219,9 +221,12 @@
         for hop in range(1, wins):
             to_win(step, piece, hop).start()
         to_rep(step, piece).start()
-        if place >= PIECES:
-            relay(items[place - PIECES])
-    for item in items[-PIECES:]:
+        if step == bands - 1 and piece + AHEAD < PIECES:
+            for later in range(1, bands):
+                to_band(later, piece + AHEAD).start()
+        if place >= LAG:
+            relay(items[place - LAG])
+    for item in items[-LAG:]:
         relay(item)
     for step, piece in items:
         if step:
@@ -239,8 +244,7 @@
     bins = lax.broadcasted_iota(jnp.int32, (share, depth), 1) % SUB
     masks = [jnp.where(bins == index, 1.0, 0.0).astype(jnp.bfloat16) for index in range(SUB)]
     for part in range(per):
-        start = (pl.program_id(0) * per + part) * 2 * SUB
-        rows = pl.ds(pl.multiple_of(start, 2 * SUB), 2 * SUB)
+        rows = slice(part * 2 * SUB, (part + 1) * 2 * SUB)
         for slot in range(slots):
             place = rep * slots + slot
             scale = jnp.where(place < counts_ref[0], 1.0 / windows, 0.0).astype(jnp.float32)
@@ -306,10 +310,12 @@
         grid_spec=pltpu.PrefetchScalarGridSpec(
             num_scalar_prefetch=2,
             grid=(-(-groups // PER),),
-            in_specs=[pl.BlockSpec(memory_space=pltpu.VMEM)],
+            in_specs=[
+                pl.BlockSpec((windows, bands, PER * 2 * SUB, LANES), lambda g, *_: (0, 0, g, 0))
+            ],
             out_specs=pl.BlockSpec((PER * SUB, slots, share, 2 * BLOCK), lambda g, *_: (g, 0, 0, 0)),
         ),
-        compiler_params=pltpu.CompilerParams(vmem_limit_bytes=40 * 2**20),
+        compiler_params=pltpu.CompilerParams(vmem_limit_bytes=605 * 2**20 // 10),
         name="cross",
     )(jnp.swapaxes(pair_blocks, 1, 2), pair_counts, everything)
 

time: 40.1 us -> 37.8 us (0.943)
  local copies, waits for them, and re-layouts: 1.27 us -> 0 us
  Pallas kernels: 37.3 us -> 36.3 us
    pallas_call x1, Pallas kernels: 29 us -> 26.8 us  [shards(): pl.pallas_call(functools.partial(spectra_kernel, (bands, wins, band_bins,...]
    unnamed x4 -> x0, local copies, waits for them, and re-layouts: 1.27 us -> none
    pallas_call x1, Pallas kernels: 8.32 us -> 9.47 us  [shards(): pl.pallas_call(functools.partial(cross_kernel, windows, share, slots, PER...]
where the time goes in v3:
time: 37.8 us; the launch traced here: 37.6 us
  Pallas kernels  36.3 us (96%)
  between operations  1.31 us (3%)
    pallas_call x1, Pallas kernels, shards(): pl.pallas_call(functools.partial(spectra_kernel, (bands, wins, band_bins,...  26.8 us
    pallas_call x1, Pallas kernels, shards(): pl.pallas_call(functools.partial(cross_kernel, windows, share, slots, PER...  9.47 us

profile of v3, /device:TPU:0, one launch (start us, length us, event | category | flops | bytes accessed | tf_op | source)
XLA Modules:
  0.0 37.6 jit_solution(5506978483943595204)
XLA Ops:
  1.3 26.8 %spectra.1.white_ref = bf16[4,4,288,128]{3,2,1,0:T(8,128)(2,1)} custom-call(s32[1]{0:T(128)S(6)} %copy.5.first_ref, bf16[2,7680,128]{2,1,0:T(8,128)(2,1)} %records_ref.1), custom_call_target="tpu_custom_call" | custom-call | tf_op jit(solution)/shard_map/spectra/pallas_call | solution.py:278
  28.1 9.5 %cross.1 = f32[136,2,64,256]{3,2,1,0:T(8,128)} custom-call(s32[1,2,4]{2,1,0:T(2,128)} %bitcast.1, s32[1]{0:T(128)S(6)} %copy.6.counts_ref, bf16[4,4,288,128]{3,2,1,0:T(8,128)(2,1)} %spectra.1.white_ref), custom_call_target="tpu_custom_call" | custom-call | tf_op jit(solution)/shard_map/cross/pallas_call | solution.py:307
